TPU v7x, 32 devices: a whole 2x2x4 slice. The times are simulated.
32 devices in a mesh: sec: 4 (over z), gx: 2 (over x), gy: 4 (over y, core).
Axes of the slice: x: 2, y: 2, z: 4, core: 2. Of those that a mesh axis runs over, the one named last changes fastest.
Arguments:
- soil_class: int32 [64, 1024], P('gx', 'gy'), may hold values from 0 to 11
- geology_class: int32 [64, 1024], P('gx', 'gy'), may hold values from 0 to 15
- land_mask: int32 [64, 1024], P('gx', 'gy'), may hold values 0 or 1
- river_mask: int32 [64, 1024], P('gx', 'gy'), may hold values 0 or 1
- elevation: float32 [64, 1024], P('gx', 'gy'), may hold values from -6 to 6
- roughness: float32 [64, 1024], P('gx', 'gy'), may hold values from 0.02 to 0.11
- rainfall: float32 [64, 1024], P('gx', 'gy'), may hold values from 0.05 to 1
- potential_evap: float32 [64, 1024], P('gx', 'gy'), may hold values from 0.05 to 0.5
- surface_head: float32 [64, 1024], P('gx', 'gy'), may hold values from -3 to 3
- pressure: float32 [8, 64, 1024], P('sec', 'gx', 'gy'), may hold values from -6 to 6
- storage: float32 [8, 64, 1024], P('sec', 'gx', 'gy'), may hold values from 0.2 to 2
- soil_embed: bfloat16 [12, 128], replicated, may hold values from -4 to 4
- geology_embed: bfloat16 [16, 128], replicated, may hold values from -4 to 4
- conv_weight: bfloat16 [3, 3, 128, 128], replicated, may hold values from -0.1875 to 0.1875
- out_weight: bfloat16 [128, 8], replicated, may hold values from -0.5 to 0.5
Outputs:
- pressure_out: float32 [8, 64, 1024], P('sec', 'gx', 'gy')
- head_out: float32 [64, 1024], P('gx', 'gy')
All inputs are finite; a program needn't handle non-finite values. No bound on the sum of `land_mask` or of `river_mask` on one device may be relied on, other than what follows from the above.
Results may differ from a plain program's by a relative error of at most 0.0041.
Values sent between devices are 32-bit elements; how exact they have to be, the bound alone decides.
A program may use at most 64 MiB of HBM per device.

v0:
```python
import functools

import jax
import jax.numpy as jnp
from jax import lax
from jax.experimental import pallas as pl
from jax.experimental.pallas import tpu as pltpu
from jax.sharding import PartitionSpec as P

SWEEPS = 4
CYCLES = 4
REACH = SWEEPS * CYCLES
LANES = 128
TAPS = 3

infil_rate = 0.3
lateral = 1.0
vertical = 0.5
F32 = jnp.float32
MESH = pl.DeviceIdType.MESH


def iota(shape, axis):
    return lax.broadcasted_iota(jnp.int32, shape, axis)


def kernel(
    geom,
    soil_ref,
    geology_ref,
    land_ref,
    river_ref,
    elevation_ref,
    roughness_ref,
    rainfall_ref,
    potential_ref,
    head_ref,
    pressure_ref,
    storage_ref,
    soil_embed_ref,
    geology_embed_ref,
    conv_ref,
    outw_ref,
    press_out,
    head_out,
    whole_in,
    real_in,
    soil_in,
    conv_in,
    in_sems,
    cls,
    fld,
    pack2,
    halo2,
    stage3,
    win3,
    pack3,
    halo3,
    shifted_cls,
    table,
    taps,
    split,
    onehot,
    cond,
    coef,
    scaled,
    inverse,
    press_a,
    press_b,
    rhs,
    surf,
    send_out,
    recv_out,
    cls_send,
    cls_recv,
    fld_send,
    fld_recv,
    p2_send,
    p2_recv,
    s3_send,
    s3_recv,
    p3_send,
    p3_recv,
    out_send,
    out_recv,
):
    n_sec, n_gx, n_gy, rows, cols, layers_dev, win_rows = geom
    layers = n_sec * layers_dev
    own = cols // n_sec
    margin = (LANES - own) // 2
    groups = LANES // margin
    s, g, h = (
        jnp.clip(lax.axis_index(name), 0, size - 1) for name, size in (("sec", n_sec), ("gx", n_gx), ("gy", n_gy))
    )
    last = n_sec - 1
    extra = 8
    deep = REACH + extra

    def aligned(value):
        return pl.multiple_of(value, 8)

    offset = REACH * g if n_gx == 2 else REACH

    def exists(dg, dh):
        return (g + dg >= 0) & (g + dg < n_gx) & (h + dh >= 0) & (h + dh < n_gy)

    surface_refs = (
        soil_ref, geology_ref, land_ref, river_ref, elevation_ref, roughness_ref, rainfall_ref, potential_ref, head_ref
    )
    surface_in = [whole_in.at[k] for k in range(4)] + [real_in.at[k] for k in range(5)]
    soil_parts = [soil_in.at[pl.ds(0, layers_dev)], soil_in.at[pl.ds(layers_dev, layers_dev)]]
    loads = [
        pltpu.make_async_copy(src, dst, in_sems.at[k])
        for k, (src, dst) in enumerate(
            zip(
                (*surface_refs, pressure_ref, storage_ref, conv_ref),
                (*surface_in, *soil_parts, conv_in),
            )
        )
    ]
    for load in loads:
        load.start()

    barrier = pltpu.get_barrier_semaphore()
    count = jnp.int32(0)
    for dg in (-1, 0, 1):
        for dh in (-1, 0, 1):
            for t in range(n_sec):
                met = exists(dg, dh)
                if dh == 0 and dg == 0:
                    met = met & (s != t)
                if dh == 1 and t != 0:
                    met = met & (s == last)
                if dh == -1 and t != last:
                    met = met & (s == 0)

                @pl.when(met)
                def _():
                    pl.semaphore_signal(
                        barrier, inc=1, device_id={"sec": t, "gx": g + dg, "gy": h + dh}, device_id_type=MESH
                    )

                count = count + met.astype(jnp.int32)

    for load in loads[:9]:
        load.wait()
    lane = iota((rows, LANES), 1)
    turn = lax.rem(margin - own * s + cols, cols)

    def window_of(values):
        return pltpu.roll(values, turn, 1)[:, :LANES]

    land = whole_in[2].astype(F32)
    rough = land * (1.0 + whole_in[3].astype(F32)) * real_in[1]
    classes = [whole_in[0].astype(F32), whole_in[1].astype(F32)]
    fields = [
        land,
        rough,
        real_in[0],
        land * real_in[2],
        land * real_in[3],
        real_in[4],
    ]
    windows = [window_of(v) for v in classes + fields]
    for k in range(2):
        cls[k, pl.ds(aligned(offset + extra), rows), :] = windows[k]
    for k in range(6):
        fld[k, pl.ds(aligned(offset), rows), :] = windows[2 + k]
    base = jnp.where(s == 0, 0, LANES - margin)
    for b in range(2):
        packed = jnp.zeros((rows, LANES), F32)
        for k in range(groups):
            moved = pltpu.roll(windows[b * groups + k], lax.rem(margin * k - base + LANES, LANES), 1)
            packed = jnp.where((lane >= margin * k) & (lane < margin * (k + 1)), moved, packed)
        pack2[b] = packed

    pl.semaphore_wait(barrier, count)

    def source_rows(dg, size):
        return pl.ds(rows - size if dg == 1 else 0, size)

    def target_rows(dg, pad, size):
        if dg == 0:
            return pl.ds(aligned(offset + pad), size)
        if dg == 1:
            return pl.ds(REACH + pad - size, size)
        return pl.ds((0 if n_gx == 2 else REACH) + rows + pad, size)

    def giver_rows(dg, pad, size):
        if dg == 1:
            return pl.ds((0 if n_gx == 2 else REACH) + pad + rows - size, size)
        return pl.ds(REACH + pad, size)

    sends = []
    recvs = {"first": [], "soil": [], "rest": []}

    def message(kind, send_when, recv_when, src, dst, recv_dst, ssem, rsem, rsem_here, target, giver):
        def copy():
            return pltpu.make_async_remote_copy(src(), dst(), ssem, rsem, device_id=target, device_id_type=MESH)

        def here():
            return pltpu.make_async_remote_copy(
                src(), recv_dst(), ssem, rsem_here, device_id=giver, device_id_type=MESH
            )

        if recv_when is not None:
            recvs[kind].append((recv_when, here))
        if send_when is not None:
            sends.append((send_when, copy))

            @pl.when(send_when)
            def _():
                copy().start()

    def surface_to(kind, dg, ref, pad, size, ssem, rsem):
        i = (dg + 1) // 2
        message(
            kind, exists(dg, 0), exists(-dg, 0),
            lambda: ref.at[:, giver_rows(dg, pad, size), :],
            lambda: ref.at[:, target_rows(dg, pad, size), :],
            lambda: ref.at[:, target_rows(dg, pad, size), :],
            ssem.at[i], rsem.at[i], rsem.at[i],
            {"sec": s, "gx": g + dg, "gy": h},
            {"sec": s, "gx": g - dg, "gy": h},
        )

    for dg in (-1, 1):
        surface_to("first", dg, cls, extra, deep, cls_send, cls_recv)

    def corner_to(side, dh, keeper, dg):
        size = rows if dg == 0 else deep
        j = dg + 1
        message(
            "first", exists(dg, dh) & (s == keeper), exists(-dg, -dh) & (s == keeper),
            lambda: pack2.at[:, source_rows(dg, size), :],
            lambda: halo2.at[:, target_rows(dg, extra, size), :],
            lambda: halo2.at[:, target_rows(dg, extra, size), :],
            p2_send.at[side * 3 + j], p2_recv.at[side * 3 + j], p2_recv.at[side * 3 + j],
            {"sec": s, "gx": g + dg, "gy": h + dh},
            {"sec": s, "gx": g - dg, "gy": h - dh},
        )

    for side, (dh, keeper) in enumerate(((1, 0), (-1, last))):
        for dg in (-1, 0, 1):
            corner_to(side, dh, keeper, dg)

    loads[9].wait()
    loads[10].wait()
    soil_blocks = [soil_in[k] for k in range(2 * layers_dev)]
    n_blocks = len(soil_blocks)
    for t in range(n_sec):
        for k in range(n_blocks):
            stage3[t, k] = pltpu.roll(soil_blocks[k], (margin - own * t) % cols, 1)[:, :LANES]
    for side, (t, edge) in enumerate(((0, 0), (last, LANES - margin))):
        packed = jnp.zeros((rows, LANES), F32)
        for k in range(n_blocks):
            moved = pltpu.roll(stage3[t, k], (margin * k - edge) % LANES, 1)
            packed = jnp.where((lane >= margin * k) & (lane < margin * (k + 1)), moved, packed)
        pack3[side] = packed
    for t in range(n_sec):

        @pl.when(s == t)
        def _():
            for k in range(n_blocks):
                win3[t, k, pl.ds(aligned(offset), rows), :] = stage3[t, k]


    def soil_to(dg, t):
        way = (dg + 1) * n_sec
        size = rows if dg == 0 else REACH
        message(
            "soil", exists(dg, 0) if dg else (s != t), exists(-dg, 0) if dg else (s != t),
            lambda: stage3.at[t, :, source_rows(dg, size), :],
            lambda: win3.at[s, :, target_rows(dg, 0, size), :],
            lambda: win3.at[t, :, target_rows(dg, 0, size), :],
            s3_send.at[way + t], s3_recv.at[way + s], s3_recv.at[way + t],
            {"sec": t, "gx": g + dg, "gy": h},
            {"sec": t, "gx": g - dg, "gy": h},
        )

    for dg in (0, -1, 1):
        for t in range(n_sec):
            soil_to(dg, t)

    def soil_edge_to(side, dh, keeper, dg, t):
        way = side * 3 + dg + 1
        size = rows if dg == 0 else REACH
        message(
            "soil", exists(dg, dh) if t == 0 else None, exists(-dg, -dh) & (s == keeper),
            lambda: pack3.at[side, source_rows(dg, size), :],
            lambda: halo3.at[s, target_rows(dg, 0, size), :],
            lambda: halo3.at[t, target_rows(dg, 0, size), :],
            p3_send.at[way], p3_recv.at[way * n_sec + s], p3_recv.at[way * n_sec + t],
            {"sec": keeper, "gx": g + dg, "gy": h + dh},
            {"sec": t, "gx": g - dg, "gy": h - dh},
        )

    for side, (dh, keeper) in enumerate(((1, 0), (-1, last))):
        for dg in (0, -1, 1):
            for t in range(n_sec):
                soil_edge_to(side, dh, keeper, dg, t)

    for dg in (-1, 1):
        surface_to("rest", dg, fld, 0, REACH, fld_send, fld_recv)

    def wait_all(kind):
        for when, copy in recvs[kind]:

            @pl.when(when)
            def _():
                copy().wait_recv()

    soil_slots = 16 * pl.cdiv(soil_embed_ref.shape[0], 16)
    geo_slots = 16 * pl.cdiv(geology_embed_ref.shape[0], 16)
    slots = soil_slots + geo_slots
    table[...] = jnp.zeros(table.shape, F32)
    table[0 : soil_embed_ref.shape[0], :] = soil_embed_ref[...].astype(F32)
    table[soil_slots : soil_slots + geology_embed_ref.shape[0], :] = geology_embed_ref[...].astype(F32)
    embed = table[...].astype(jnp.bfloat16)
    loads[11].wait()
    taps[...] = jnp.zeros(taps.shape, F32)
    for i in range(TAPS):
        for j in range(TAPS):
            at = (i * TAPS + j) * slots
            taps[at : at + slots, :] = jnp.dot(embed, conv_in[i, j], preferred_element_type=F32)
    channels = conv_ref.shape[3]
    depth = TAPS * TAPS * slots
    for k in range(taps.shape[0] // LANES):
        turned = taps[k * LANES : (k + 1) * LANES, :].T
        upper = turned.astype(jnp.bfloat16)
        split[0:channels, k * LANES : (k + 1) * LANES] = upper
        split[channels : 2 * channels, k * LANES : (k + 1) * LANES] = (turned - upper.astype(F32)).astype(
            jnp.bfloat16
        )
    outw_t = outw_ref[...]

    wait_all("first")

    edge_at = jnp.where(s == 0, 0, LANES - margin)

    def edge_mask(shape):
        at = iota(shape, 1)
        return ((s == 0) & (at < margin)) | ((s == last) & (at >= LANES - margin))

    def on_grid(shape, first):
        row = g * rows - offset + first + iota(shape, 0)
        col = h * cols + s * own - margin + iota(shape, 1)
        return (row >= 0) & (row < n_gx * rows) & (col >= 0) & (col < n_gy * cols)

    def unpack(packed, k):
        return pltpu.roll(packed, lax.rem(edge_at - margin * k + LANES, LANES), 1)

    tall = (win_rows + 2 * extra, LANES)
    tall_edge = edge_mask(tall)
    tall_grid = on_grid(tall, -extra)
    for k in range(2):
        merged = jnp.where(tall_edge, unpack(halo2[0], k), cls[k])
        merged = jnp.where(tall_grid, merged, -100.0)
        for j in range(TAPS):
            shifted_cls[j, k] = merged if j == 1 else pltpu.roll(merged, (1 - j) % LANES, 1)

    group = 8

    def make_onehot(it, carry):
        for j in range(TAPS):
            soil_rows = shifted_cls[j, 0, pl.ds(aligned(it * group), group), :]
            geo_rows = shifted_cls[j, 1, pl.ds(aligned(it * group), group), :]
            for k in range(group):
                at = pl.multiple_of(((it * group + k) * TAPS + j) * slots, 16)
                soil_hot = iota((soil_slots, LANES), 0).astype(F32) == soil_rows[k : k + 1]
                geo_hot = iota((geo_slots, LANES), 0).astype(F32) == geo_rows[k : k + 1]
                hot = jnp.concatenate([soil_hot, geo_hot], axis=0)
                onehot[pl.ds(at, slots), :] = jnp.where(hot, 1.0, 0.0).astype(jnp.bfloat16)
        return carry

    lax.fori_loop(0, tall[0] // group, make_onehot, 0)

    def convolve(it, carry):
        r = it * group
        parts = [
            onehot[pl.ds(pl.multiple_of((r + k + extra - 1) * TAPS * slots, 16), depth), :] for k in range(group)
        ]
        both = jnp.dot(split[:, :depth], jnp.concatenate(parts, axis=1), preferred_element_type=F32)
        hidden = jnp.maximum(both[:channels] + both[channels:], 0.0).astype(jnp.bfloat16)
        found = jnp.dot(outw_t, hidden, preferred_element_type=F32)
        stacked = jnp.stack([found[:, k * LANES : (k + 1) * LANES] for k in range(group)], axis=0)
        cond[:, pl.ds(aligned(r), group), :] = jnp.swapaxes(stacked, 0, 1)
        return carry

    lax.fori_loop(0, win_rows // group, convolve, 0)

    flat = (win_rows, LANES)
    grid_mask = on_grid(flat, 0)
    edge = edge_mask(flat)
    row_at = iota(flat, 0)
    lane_at = iota(flat, 1)
    usable = grid_mask & (lane_at > 0) & (lane_at < LANES - 1)
    for l in range(layers):
        cond[l] = jnp.where(usable, jnp.exp(cond[l]), 0.0)

    def north(v):
        return pltpu.roll(v, 1, 0)

    def south(v):
        return pltpu.roll(v, win_rows - 1, 0)

    def east(v):
        return pltpu.roll(v, LANES - 1, 1)

    def west(v):
        return pltpu.roll(v, 1, 1)

    first_row = row_at == 0
    final_row = row_at == win_rows - 1

    def north0(v):
        return jnp.where(first_row, 0.0, north(v))

    def south0(v):
        return jnp.where(final_row, 0.0, south(v))

    wait_all("rest")

    def field(k):
        b, at = (k + 2) // groups, (k + 2) % groups
        merged = jnp.where(edge, unpack(halo2[b, extra : extra + win_rows, :], at), fld[k])
        return jnp.where(grid_mask, merged, 0.0)

    land_w, rough_w, elev_w, rain_w, potential_w, head_w = [field(k) for k in range(6)]
    top_cond = cond[0]
    surf[0] = land_w * (infil_rate * top_cond / (1.0 + top_cond))
    surf[1] = potential_w
    surf[2] = rain_w
    surf[3] = elev_w
    surf[4] = head_w
    total = jnp.zeros(flat, F32)
    for k, move in enumerate((north0, south0, east, west)):
        way = land_w * 0.5 * (rough_w + move(rough_w))
        total = total + way
        surf[5 + k] = way
    surf[9] = total

    wait_all("soil")

    for l in range(layers):
        t, k = l // layers_dev, l % layers_dev
        press = jnp.where(edge, unpack(halo3[t], k), win3[t, k])
        store = jnp.where(edge, unpack(halo3[t], layers_dev + k), win3[t, layers_dev + k])
        press_a[l] = jnp.where(grid_mask, press, 0.0)
        mid = cond[l]
        up = vertical * 0.5 * (mid + cond[l - 1]) if l > 0 else vertical * 0.5 * mid
        down = vertical * 0.5 * (mid + cond[l + 1]) if l < layers - 1 else vertical * 0.5 * mid
        sides = [lateral * 0.5 * (mid + move(mid)) for move in (north0, south0, east, west)]
        diagonal = store + up + down + sides[0] + sides[1] + sides[2] + sides[3]
        inv = jnp.where(grid_mask, 1.0 / jnp.where(grid_mask, diagonal, 1.0), 0.0)
        inverse[l] = inv
        scaled[l] = jnp.where(grid_mask, store, 0.0) * inv
        coef[0, l] = up * inv
        coef[1, l] = down * inv
        coef[2, l] = jnp.where(first_row, 0.0, sides[0] * inv)
        coef[3, l] = jnp.where(final_row, 0.0, sides[1] * inv)
        coef[4, l] = sides[2] * inv
        coef[5, l] = sides[3] * inv

    def sweep(src, dst):
        for l in range(layers):
            mid = src[l]
            new = rhs[l] + coef[2, l] * north(mid) + coef[3, l] * south(mid)
            new = new + coef[4, l] * east(mid) + coef[5, l] * west(mid)
            if l > 0:
                new = new + coef[0, l] * src[l - 1]
            if l < layers - 1:
                new = new + coef[1, l] * src[l + 1]
            dst[l] = new

    def cycle(c, carry):
        top = press_a[0]
        head = surf[4]
        infil = surf[0] * (head - top)
        evap = surf[1] * jax.nn.sigmoid(top)
        level = head + surf[3]
        flux = surf[5] * north0(level) + surf[6] * south0(level)
        flux = flux + surf[7] * east(level) + surf[8] * west(level) - surf[9] * level
        surf[4] = head + (surf[2] - infil + flux)
        for l in range(layers):
            rhs[l] = scaled[l] * press_a[l]
        rhs[0] = rhs[0] + inverse[0] * (infil - evap)

        def pair(i, inner):
            sweep(press_a, press_b)
            sweep(press_b, press_a)
            return inner

        return lax.fori_loop(0, SWEEPS // 2, pair, carry)

    lax.fori_loop(0, CYCLES, cycle, 0)

    mine = pl.ds(aligned(offset), rows)
    low = lane < own
    half = rows // layers_dev
    final_head = surf[4, mine, :]
    head_pack = jnp.where(
        low[:half],
        pltpu.roll(final_head[:half], LANES - margin, 1),
        pltpu.roll(final_head[half:], margin, 1),
    )
    for t in range(n_sec):
        send_out[t, 0:rows, :] = jnp.where(
            low,
            pltpu.roll(press_a[layers_dev * t, mine, :], LANES - margin, 1),
            pltpu.roll(press_a[layers_dev * t + 1, mine, :], margin, 1),
        )
        send_out[t, rows : rows + half, :] = head_pack

    def result_to(t, source):
        return pltpu.make_async_remote_copy(
            send_out.at[t], recv_out.at[source], out_send.at[t], out_recv.at[source],
            device_id={"sec": t, "gx": g, "gy": h}, device_id_type=MESH,
        )

    for t in range(n_sec):

        @pl.when(s != t)
        def _():
            result_to(t, s).start()

    for t in range(n_sec):

        @pl.when(s == t)
        def _():
            recv_out[t] = send_out[t]

    for when, copy in sends:

        @pl.when(when)
        def _():
            copy().wait_send()

    for t in range(n_sec):

        @pl.when(s != t)
        def _():
            result_to(t, t).wait()

    wide = iota((rows + half, LANES), 1) < own
    for m in range(cols // LANES):
        left, right = recv_out[2 * m], recv_out[2 * m + 1]
        even = jnp.where(wide, left, pltpu.roll(right, own, 1))
        odd = jnp.where(wide, pltpu.roll(left, own, 1), right)
        at = slice(m * LANES, (m + 1) * LANES)
        press_out[0, :, at] = even[:rows]
        press_out[1, :, at] = odd[:rows]
        head_out[0:half, at] = even[rows:]
        head_out[half:rows, at] = odd[rows:]


def shards(*args):
    pressure, soil_embed, geology_embed, conv_weight, out_weight = (args[i] for i in (9, 11, 12, 13, 14))
    n_sec, n_gx, n_gy = (lax.axis_size(name) for name in ("sec", "gx", "gy"))
    layers_dev, rows, cols = pressure.shape
    layers = layers_dev * n_sec
    own = cols // n_sec
    margin = (LANES - own) // 2
    assert margin > REACH and layers_dev * own == LANES and 2 * layers_dev * margin == LANES
    assert n_gx >= 2 and rows >= REACH + 8 and layers_dev == 2
    win_rows = rows + (REACH if n_gx == 2 else 2 * REACH)
    channels = conv_weight.shape[3]
    slots = 16 * pl.cdiv(soil_embed.shape[0], 16) + 16 * pl.cdiv(geology_embed.shape[0], 16)
    depth = TAPS * TAPS * slots
    deep = LANES * pl.cdiv(depth, LANES)
    geom = (n_sec, n_gx, n_gy, rows, cols, layers_dev, win_rows)
    vmem = pltpu.VMEM
    dma = pltpu.SemaphoreType.DMA
    bf16 = jnp.bfloat16
    tall = win_rows + 16
    column = (layers, win_rows, LANES)
    scratch = [
        vmem((4, rows, cols), jnp.int32),
        vmem((5, rows, cols), F32),
        vmem((2 * layers_dev, rows, cols), F32),
        vmem(conv_weight.shape, bf16),
        dma((12,)),
        vmem((2, tall, LANES), F32),
        vmem((6, win_rows, LANES), F32),
        vmem((2, rows, LANES), F32),
        vmem((2, tall, LANES), F32),
        vmem((n_sec, 2 * layers_dev, rows, LANES), F32),
        vmem((n_sec, 2 * layers_dev, win_rows, LANES), F32),
        vmem((2, rows, LANES), F32),
        vmem((n_sec, win_rows, LANES), F32),
        vmem((TAPS, 2, tall, LANES), F32),
        vmem((slots, channels), F32),
        vmem((deep, channels), F32),
        vmem((2 * channels, deep), bf16),
        vmem((tall * TAPS * slots, LANES), bf16),
        vmem(column, F32),
        vmem((6,) + column, F32),
        vmem(column, F32),
        vmem(column, F32),
        vmem(column, F32),
        vmem(column, F32),
        vmem(column, F32),
        vmem((10, win_rows, LANES), F32),
        vmem((n_sec, rows + rows // layers_dev, LANES), F32),
        vmem((n_sec, rows + rows // layers_dev, LANES), F32),
        dma((2,)),
        dma((2,)),
        dma((2,)),
        dma((2,)),
        dma((6,)),
        dma((6,)),
        dma((3 * n_sec,)),
        dma((3 * n_sec,)),
        dma((6,)),
        dma((6 * n_sec,)),
        dma((n_sec,)),
        dma((n_sec,)),
    ]
    return pl.pallas_call(
        functools.partial(kernel, geom),
        out_shape=(
            jax.ShapeDtypeStruct(pressure.shape, F32),
            jax.ShapeDtypeStruct((rows, cols), F32),
        ),
        in_specs=[pl.BlockSpec(memory_space=vmem if k in (11, 12, 14) else pl.ANY) for k in range(len(args))],
        out_specs=(pl.BlockSpec(memory_space=vmem), pl.BlockSpec(memory_space=vmem)),
        scratch_shapes=scratch,
        compiler_params=pltpu.CompilerParams(
            collective_id=0, has_side_effects=True, vmem_limit_bytes=62 * 1024 * 1024
        ),
    )(*args[:14], out_weight.T)


def solution(mesh):
    in_specs = (P("gx", "gy"),) * 9 + (P("sec", "gx", "gy"),) * 2 + (P(),) * 4
    out_specs = (P("sec", "gx", "gy"), P("gx", "gy"))
    return jax.shard_map(shards, mesh=mesh, in_specs=in_specs, out_specs=out_specs, check_vma=False)
```

profile of v0, /device:TPU:1, one launch (start us, length us, event | category | flops | bytes accessed | tf_op | source)
XLA Modules:
  0.0 29.4 jit_solution(13992400993166769121)
XLA Ops:
  0.6 26.6 %shard_map.158 = (f32[2,32,256]{2,1,0:T(8,128)}, f32[32,256]{1,0:T(8,128)}) custom-call(s32[32,256]{1,0:T(8,128)} %soil_ref.1, s32[32,256]{1,0:T(8,128)} %geology_ref.1, s32[32,256]{1,0:T(8,128)} %land_ref.1, s32[32,256]{1,0:T(8,128)} %river_ref.1, f32[32,256]{1,0:T(8,128)} %elevation_ref.1, f32[32,256]{1,0:T(8,128)} %roughness_ref.1, ...), custom_call_target="tpu_custom_call" | custom-call | tf_op jit(solution)/shard_map/pallas_call | solution.py:619
  27.3 0.0 copy-start
  27.3 1.5 %copy.19 = f32[2,32,256]{2,1,0:T(8,128)} copy(f32[2,32,256]{2,1,0:T(8,128)} %get-tuple-element.4) | data formatting | bytes 131072
  28.7 0.0 copy-done
  28.8 0.6 %copy.20 = f32[32,256]{1,0:T(8,128)} copy(f32[32,256]{1,0:T(8,128)S(1)} %copy-done) | data formatting | bytes 65536
Async XLA Ops:
  27.3 1.5 %copy-start = (f32[32,256]{1,0:T(8,128)S(1)}, f32[32,256]{1,0:T(8,128)}, u32[]{:S(2)}) copy-start(f32[32,256]{1,0:T(8,128)} %get-tuple-element.5) | copy-start | bytes 98308
where the time goes:
time: 29.6 us; the launch traced here: 29.4 us
  Pallas kernels  26.6 us (90%)
  local copies, waits for them, and re-layouts  2.1 us (7%)
  between operations  0.65 us (2%)
    pallas_call x1, Pallas kernels, shards(): pl.pallas_call(functools.partial(kernel, geom), out_shape=(jax.ShapeDtype...  26.6 us
    unnamed x4, local copies, waits for them, and re-layouts  2.1 us

commit v1 on v0

--- a/solution.py
+++ b/solution.py
@@ -89,6 +89,9 @@
     own = cols // n_sec
     margin = (LANES - own) // 2
     groups = LANES // margin
+    keep = own + 2 * REACH
+    low_lane = margin - REACH
+    piece = LANES - keep
     s, g, h = (
         jnp.clip(lax.axis_index(name), 0, size - 1) for name, size in (("sec", n_sec), ("gx", n_gx), ("gy", n_gy))
     )
@@ -244,26 +247,32 @@
         for dg in (-1, 0, 1):
             corner_to(side, dh, keeper, dg)
 
+    for dg in (-1, 1):
+        surface_to("rest", dg, fld, 0, REACH, fld_send, fld_recv)
+
     loads[9].wait()
     loads[10].wait()
     soil_blocks = [soil_in[k] for k in range(2 * layers_dev)]
     n_blocks = len(soil_blocks)
+    sides3 = {0: (0, 0), last: (1, LANES - margin)}
     for t in range(n_sec):
-        for k in range(n_blocks):
-            stage3[t, k] = pltpu.roll(soil_blocks[k], (margin - own * t) % cols, 1)[:, :LANES]
-    for side, (t, edge) in enumerate(((0, 0), (last, LANES - margin))):
-        packed = jnp.zeros((rows, LANES), F32)
-        for k in range(n_blocks):
-            moved = pltpu.roll(stage3[t, k], (margin * k - edge) % LANES, 1)
-            packed = jnp.where((lane >= margin * k) & (lane < margin * (k + 1)), moved, packed)
-        pack3[side] = packed
+        blocks = [pltpu.roll(v, (margin - own * t) % cols, 1)[:, :LANES] for v in soil_blocks]
+        for j in range(n_blocks - 1):
+            moved = pltpu.roll(blocks[-1], (keep - piece * j) % LANES, 1)
+            stage3[t, j] = jnp.where((lane >= low_lane) & (lane < low_lane + keep), blocks[j], moved)
+        if t in sides3:
+            side, edge = sides3[t]
+            packed = jnp.zeros((rows, LANES), F32)
+            for k in range(n_blocks):
+                moved = pltpu.roll(blocks[k], (margin * k - edge) % LANES, 1)
+                packed = jnp.where((lane >= margin * k) & (lane < margin * (k + 1)), moved, packed)
+            pack3[side] = packed
     for t in range(n_sec):
 
         @pl.when(s == t)
         def _():
-            for k in range(n_blocks):
-                win3[t, k, pl.ds(aligned(offset), rows), :] = stage3[t, k]
-
+            for j in range(n_blocks - 1):
+                win3[t, j, pl.ds(aligned(offset), rows), :] = stage3[t, j]
 
     def soil_to(dg, t):
         way = (dg + 1) * n_sec
@@ -299,9 +308,6 @@
         for dg in (0, -1, 1):
             for t in range(n_sec):
                 soil_edge_to(side, dh, keeper, dg, t)
-
-    for dg in (-1, 1):
-        surface_to("rest", dg, fld, 0, REACH, fld_send, fld_recv)
 
     def wait_all(kind):
         for when, copy in recvs[kind]:
@@ -442,19 +448,31 @@
 
     wait_all("soil")
 
+    soil_mask = grid_mask & (lane_at >= low_lane) & (lane_at < low_lane + keep)
+
+    def soil_block(t, k):
+        if k < n_blocks - 1:
+            found = win3[t, k]
+        else:
+            found = pltpu.roll(win3[t, 0], (-keep) % LANES, 1)
+            for j in range(1, n_blocks - 1):
+                back = pltpu.roll(win3[t, j], (piece * j - keep) % LANES, 1)
+                found = jnp.where(lane_at < low_lane + piece * j, found, back)
+        return jnp.where(edge, unpack(halo3[t], k), found)
+
     for l in range(layers):
         t, k = l // layers_dev, l % layers_dev
-        press = jnp.where(edge, unpack(halo3[t], k), win3[t, k])
-        store = jnp.where(edge, unpack(halo3[t], layers_dev + k), win3[t, layers_dev + k])
-        press_a[l] = jnp.where(grid_mask, press, 0.0)
+        press = soil_block(t, k)
+        store = soil_block(t, layers_dev + k)
+        press_a[l] = jnp.where(soil_mask, press, 0.0)
         mid = cond[l]
         up = vertical * 0.5 * (mid + cond[l - 1]) if l > 0 else vertical * 0.5 * mid
         down = vertical * 0.5 * (mid + cond[l + 1]) if l < layers - 1 else vertical * 0.5 * mid
         sides = [lateral * 0.5 * (mid + move(mid)) for move in (north0, south0, east, west)]
         diagonal = store + up + down + sides[0] + sides[1] + sides[2] + sides[3]
-        inv = jnp.where(grid_mask, 1.0 / jnp.where(grid_mask, diagonal, 1.0), 0.0)
+        inv = jnp.where(soil_mask, 1.0 / jnp.where(soil_mask, diagonal, 1.0), 0.0)
         inverse[l] = inv
-        scaled[l] = jnp.where(grid_mask, store, 0.0) * inv
+        scaled[l] = jnp.where(soil_mask, store, 0.0) * inv
         coef[0, l] = up * inv
         coef[1, l] = down * inv
         coef[2, l] = jnp.where(first_row, 0.0, sides[0] * inv)
@@ -562,6 +580,7 @@
     own = cols // n_sec
     margin = (LANES - own) // 2
     assert margin > REACH and layers_dev * own == LANES and 2 * layers_dev * margin == LANES
+    assert (LANES - own - 2 * REACH) * 2 * layers_dev == LANES
     assert n_gx >= 2 and rows >= REACH + 8 and layers_dev == 2
     win_rows = rows + (REACH if n_gx == 2 else 2 * REACH)
     channels = conv_weight.shape[3]
@@ -584,8 +603,8 @@
         vmem((6, win_rows, LANES), F32),
         vmem((2, rows, LANES), F32),
         vmem((2, tall, LANES), F32),
-        vmem((n_sec, 2 * layers_dev, rows, LANES), F32),
-        vmem((n_sec, 2 * layers_dev, win_rows, LANES), F32),
+        vmem((n_sec, 2 * layers_dev - 1, rows, LANES), F32),
+        vmem((n_sec, 2 * layers_dev - 1, win_rows, LANES), F32),
         vmem((2, rows, LANES), F32),
         vmem((n_sec, win_rows, LANES), F32),
         vmem((TAPS, 2, tall, LANES), F32),

time: 29.6 us -> 27.7 us (0.936)
  Pallas kernels: 26.6 us -> 24.7 us
    pallas_call x1, Pallas kernels: 26.6 us -> 24.7 us  [shards(): pl.pallas_call(functools.partial(kernel, geom), out_shape=(jax.ShapeDtype...]
where the time goes in v1:
time: 27.7 us; the launch traced here: 27.5 us
  Pallas kernels  24.7 us (89%)
  local copies, waits for them, and re-layouts  2.1 us (8%)
  between operations  0.65 us (2%)
    pallas_call x1, Pallas kernels, shards(): pl.pallas_call(functools.partial(kernel, geom), out_shape=(jax.ShapeDtype...  24.7 us
    unnamed x4, local copies, waits for them, and re-layouts  2.1 us

profile of v1, /device:TPU:1, one launch (start us, length us, event | category | flops | bytes accessed | tf_op | source)
XLA Modules:
  0.0 27.5 jit_solution(9146590143160824885)
XLA Ops:
  0.6 24.7 %shard_map.158 = (f32[2,32,256]{2,1,0:T(8,128)}, f32[32,256]{1,0:T(8,128)}) custom-call(s32[32,256]{1,0:T(8,128)} %soil_ref.1, s32[32,256]{1,0:T(8,128)} %geology_ref.1, s32[32,256]{1,0:T(8,128)} %land_ref.1, s32[32,256]{1,0:T(8,128)} %river_ref.1, f32[32,256]{1,0:T(8,128)} %elevation_ref.1, f32[32,256]{1,0:T(8,128)} %roughness_ref.1, ...), custom_call_target="tpu_custom_call" | custom-call | tf_op jit(solution)/shard_map/pallas_call | solution.py:638
  25.4 0.0 copy-start
  25.4 1.5 %copy.19 = f32[2,32,256]{2,1,0:T(8,128)} copy(f32[2,32,256]{2,1,0:T(8,128)} %get-tuple-element.4) | data formatting | bytes 131072
  26.8 0.0 copy-done
  26.8 0.6 %copy.20 = f32[32,256]{1,0:T(8,128)} copy(f32[32,256]{1,0:T(8,128)S(1)} %copy-done) | data formatting | bytes 65536
Async XLA Ops:
  25.4 1.5 %copy-start = (f32[32,256]{1,0:T(8,128)S(1)}, f32[32,256]{1,0:T(8,128)}, u32[]{:S(2)}) copy-start(f32[32,256]{1,0:T(8,128)} %get-tuple-element.5) | copy-start | bytes 98308

commit v2 on v1

--- a/solution.py
+++ b/solution.py
@@ -287,7 +287,7 @@
             {"sec": t, "gx": g - dg, "gy": h},
         )
 
-    for dg in (0, -1, 1):
+    for dg in (-1, 1, 0):
         for t in range(n_sec):
             soil_to(dg, t)
 

time: 27.7 us -> 27.6 us (level)
  no operation moved by 1% of the time
where the time goes in v2:
time: 27.6 us; the launch traced here: 27.4 us
  Pallas kernels  24.7 us (89%)
  local copies, waits for them, and re-layouts  2.1 us (8%)
  between operations  0.65 us (2%)
    pallas_call x1, Pallas kernels, shards(): pl.pallas_call(functools.partial(kernel, geom), out_shape=(jax.ShapeDtype...  24.7 us
    unnamed x4, local copies, waits for them, and re-layouts  2.1 us

profile of v2, /device:TPU:1, one launch (start us, length us, event | category | flops | bytes accessed | tf_op | source)
XLA Modules:
  0.0 27.4 jit_solution(13033301108047570052)
XLA Ops:
  0.6 24.7 %shard_map.158 = (f32[2,32,256]{2,1,0:T(8,128)}, f32[32,256]{1,0:T(8,128)}) custom-call(s32[32,256]{1,0:T(8,128)} %soil_ref.1, s32[32,256]{1,0:T(8,128)} %geology_ref.1, s32[32,256]{1,0:T(8,128)} %land_ref.1, s32[32,256]{1,0:T(8,128)} %river_ref.1, f32[32,256]{1,0:T(8,128)} %elevation_ref.1, f32[32,256]{1,0:T(8,128)} %roughness_ref.1, ...), custom_call_target="tpu_custom_call" | custom-call | tf_op jit(solution)/shard_map/pallas_call | solution.py:638
  25.3 0.0 copy-start
  25.3 1.5 %copy.19 = f32[2,32,256]{2,1,0:T(8,128)} copy(f32[2,32,256]{2,1,0:T(8,128)} %get-tuple-element.4) | data formatting | bytes 131072
  26.8 0.0 copy-done
  26.8 0.6 %copy.20 = f32[32,256]{1,0:T(8,128)} copy(f32[32,256]{1,0:T(8,128)S(1)} %copy-done) | data formatting | bytes 65536
Async XLA Ops:
  25.3 1.5 %copy-start = (f32[32,256]{1,0:T(8,128)S(1)}, f32[32,256]{1,0:T(8,128)}, u32[]{:S(2)}) copy-start(f32[32,256]{1,0:T(8,128)} %get-tuple-element.5) | copy-start | bytes 98308
